TPU v7x, 32 devices: a whole 2x2x4 slice. The times are simulated.
32 devices in a mesh: wide: 8 (over z, y), narrow: 4 (over x, core).
Axes of the slice: x: 2, y: 2, z: 4, core: 2. Of those that a mesh axis runs over, the one named last changes fastest.
Arguments:
- tokens: bfloat16 [98304, 768], P(('wide', 'narrow')), may hold values from -6 to 6
- labels: int32 [96], P(('wide', 'narrow')), may hold values from 0 to 2
- qkv_weight: bfloat16 [768, 2304], replicated, may hold values from -0.21875 to 0.21875
- out_weight: bfloat16 [768, 768], replicated, may hold values from -1.75 to 1.75
- up_weight: bfloat16 [768, 3072], replicated, may hold values from -0.21875 to 0.21875
- down_weight: bfloat16 [3072, 768], replicated, may hold values from -0.109375 to 0.109375
- ffn_bias: float32 [3072], replicated, may hold values from -4 to 4
- layer_biases: float32 [6, 768], replicated, may hold values from -4 to 4
- norm_gains: float32 [2, 768], replicated, may hold values from 0.5 to 1.5
- pool_weight: float32 [768, 768], replicated, may hold values from -0.21875 to 0.21875
- pool_moment: float32 [768, 768], replicated, may hold values from -3 to 3
- class_weight: float32 [768, 3], replicated, may hold values from -0.21875 to 0.21875
- class_moment: float32 [768, 3], replicated, may hold values from -20 to 20
- ramp_biases: float32 [771], replicated, may hold values from -3 to 3
- bias_moment: float32 [771], replicated, may hold values from -6 to 6
- start_factor: float32 [768, 8], replicated, may hold values from -6 to 6
- error_buffer: float32 [24576, 768], P(('wide', 'narrow')), may hold values from -0.75 to 0.75
Outputs:
- layer_out: bfloat16 [98304, 768], P(('wide', 'narrow'))
- pool_moment_new: float32 [768, 768], replicated
- pool_weight_new: float32 [768, 768], replicated
- class_moment_new: float32 [768, 3], replicated
- class_weight_new: float32 [768, 3], replicated
- bias_moment_new: float32 [771], replicated
- ramp_biases_new: float32 [771], replicated
- error_new: float32 [24576, 768], P(('wide', 'narrow'))
- factor_new: float32 [768, 8], replicated
All inputs are finite; a program needn't handle non-finite values.
Results may differ from a plain program's by a relative error of at most 0.012.
Values sent between devices are 32-bit elements; how exact they have to be, the bound alone decides.
A program may use at most 192 MiB of HBM per device.

v0:
```python
import functools

import jax
import jax.numpy as jnp
from jax import lax
from jax.experimental import pallas as pl
from jax.experimental.pallas import tpu as pltpu
from jax.sharding import PartitionSpec as P

HEAD_DIM = 64
SEQ_LEN = 1024
PAIR = 128
V_ROWS = 80
ROW_TILE = 16
LANES = 128
SLICE = 128
LATE_STEPS = 2
HEAD_GROUP = 4
LOG2E = 1.4426950408889634
SAFE = 2.0**100
MOMENTUM = 0.9
RATE_POOL = 0.03
RATE_HEAD = 0.002
RATE_BIAS = 0.03
MIB = 1024 * 1024
ATTENTION_MIB = 23
RAMP_MIB = 12
FINISH_MIB = 14

f32 = jnp.float32
bf16 = jnp.bfloat16
NT = ((1,), (1,))
TN = ((0,), (0,))


def in_hbm(array):
    return pltpu.with_memory_space_constraint(array, pltpu.HBM)


def dot(left, right, contract=((1,), (0,))):
    return lax.dot_general(left, right, (contract, ((), ())), preferred_element_type=f32)


def norm_rows(values, gain, shift):
    centred = values - jnp.mean(values, -1, keepdims=True)
    variance = jnp.mean(centred * centred, -1, keepdims=True)
    return centred * lax.rsqrt(variance + 1e-12) * gain + shift


def gelu(values):
    half = 0.5 * values
    return half * lax.erf(values * 0.7071067811865476) + half


def head_sums(scores, values_aug, shifted):
    if shifted:
        scores = scores - jnp.max(scores, 0, keepdims=True)
    return dot(values_aug, jnp.exp2(scores * LOG2E).astype(bf16))


def put_context(context_t, head, sums):
    scale = 1.0 / sums[HEAD_DIM : HEAD_DIM + 8]
    groups = [sums[g : g + 8] * scale for g in range(0, HEAD_DIM, 8)]
    rows = pl.ds(pl.multiple_of(head * HEAD_DIM, HEAD_DIM), HEAD_DIM)
    context_t[rows, :] = jnp.concatenate(groups, 0).astype(bf16)


def attention_kernel(carried, tokens, qkv_weight, layer_biases, *refs):
    sources, (sequences, context), targets = (
        refs[:carried],
        refs[carried : carried + 2],
        refs[carried + 2 :][:carried],
    )
    (
        key_weight,
        query_weight_t,
        value_weight_t,
        query_bias,
        value_bias,
        keys,
        queries_t,
        values_t,
        context_t,
        low,
        high,
        weight_sem,
        token_sem,
        carry_sem,
    ) = refs[2 * carried + 2 :]
    step = pl.program_id(0)
    steps = pl.num_programs(0)
    length, width = queries_t.shape[2], tokens.shape[1]
    heads = width // HEAD_DIM

    def weight_copy(index, into):
        columns = qkv_weight.at[:, pl.ds(index * width, width)]
        return pltpu.make_async_copy(columns, into, weight_sem.at[index])

    def rows_of(index):
        return pl.ds(pl.multiple_of(index * length, length), length)

    def token_copy(index):
        rows = rows_of(index)
        return pltpu.make_async_copy(tokens.at[rows], sequences.at[rows], token_sem.at[index])

    carries = [
        pltpu.make_async_copy(source, target, carry_sem.at[index])
        for index, (source, target) in enumerate(zip(sources, targets, strict=True))
    ]
    query_weight = context.at[pl.ds(0, width)]
    value_weight = context.at[pl.ds(width, width)]
    query_copy = weight_copy(0, query_weight)
    key_copy = weight_copy(1, key_weight)
    value_copy = weight_copy(2, value_weight)

    @pl.when(step == 0)
    def _():
        query_copy.start()
        value_copy.start()
        token_copy(0).start()
        key_copy.start()
        columns = jnp.concatenate([layer_biases[...], jnp.zeros((2, width), f32)], 0).T
        query_bias[...] = jnp.broadcast_to(columns[:, 0:1], (width, LANES))
        value_bias[...] = jnp.broadcast_to(columns[:, 1:2], (width, LANES))
        queries_t[...] = jnp.zeros_like(queries_t)
        values_t[:, HEAD_DIM:, :] = jnp.ones((heads, V_ROWS - HEAD_DIM, length), bf16)
        query_copy.wait()
        query_weight_t[...] = query_weight[...].T
        value_copy.wait()
        value_weight_t[...] = value_weight[...].T
        key_copy.wait()
        @pl.loop(1, steps)
        def _(index):
            token_copy(index).start()

        for copy in carries:
            copy.start()

    token_copy(step).wait()

    def wide_bias(bias):
        return jnp.concatenate([bias[...]] * (length // LANES), 1)

    sequence = sequences[rows_of(step), :]
    key_rows = dot(sequence, key_weight[...]).astype(bf16)
    for pair in range(heads // 2):
        keys[pair] = key_rows[:, pair * PAIR : (pair + 1) * PAIR]

    query_cols = ((dot(query_weight_t[...], sequence, NT) + wide_bias(query_bias)) * 0.125).astype(bf16)
    value_cols = (dot(value_weight_t[...], sequence, NT) + wide_bias(value_bias)).astype(bf16)
    for head in range(heads):
        own = slice(head * HEAD_DIM, (head + 1) * HEAD_DIM)
        half = (head % 2) * HEAD_DIM
        queries_t[head, half : half + HEAD_DIM, :] = query_cols[own]
        values_t[head, :HEAD_DIM, :] = value_cols[own]

    low[...] = jnp.ones_like(low)
    high[...] = jnp.ones_like(high)

    @pl.loop(0, heads // HEAD_GROUP)
    def _(group):
        for offset in range(HEAD_GROUP):
            head = group * HEAD_GROUP + offset
            sums = head_sums(dot(keys[head // 2], queries_t[head]), values_t[head], False)
            denominators = sums[HEAD_DIM : HEAD_DIM + 8]
            low[...] = jnp.minimum(low[...], denominators)
            high[...] = jnp.maximum(high[...], denominators)
            put_context(context_t, head, sums)
            if offset % 2:
                lanes = pl.ds(pl.multiple_of((head // 2) * PAIR, PAIR), PAIR)
                context[rows_of(step), lanes] = context_t[lanes, :].T

    in_range = (jnp.min(low[...]) > 1.0 / SAFE) & (jnp.max(high[...]) < SAFE)

    @pl.when(jnp.logical_not(in_range))
    def _():
        @pl.loop(0, heads)
        def _(head):
            sums = head_sums(dot(keys[head // 2], queries_t[head]), values_t[head], True)
            put_context(context_t, head, sums)

        context[rows_of(step), :] = context_t[...].T

    @pl.when(step == steps - 1)
    def _():
        for copy in carries:
            copy.wait()


def attention(tokens, qkv_weight, layer_biases, carried):
    rows, width = tokens.shape
    count = rows // SEQ_LEN
    heads = width // HEAD_DIM
    hbm = pl.BlockSpec(memory_space=pltpu.HBM)
    square = pltpu.VMEM((width, width), bf16)
    return pl.pallas_call(
        functools.partial(attention_kernel, len(carried)),
        grid=(count,),
        in_specs=[hbm, hbm, pl.BlockSpec((6, width), lambda i: (0, 0))] + [hbm] * len(carried),
        out_specs=[pl.BlockSpec(memory_space=pltpu.VMEM)] * (2 + len(carried)),
        out_shape=[pltpu.VMEM(array.shape, array.dtype) for array in (tokens, tokens, *carried)],
        scratch_shapes=[square] * 3
        + [
            pltpu.VMEM((width, LANES), f32),
            pltpu.VMEM((width, LANES), f32),
            pltpu.VMEM((heads // 2, SEQ_LEN, PAIR), bf16),
            pltpu.VMEM((heads, PAIR, SEQ_LEN), bf16),
            pltpu.VMEM((heads, V_ROWS, SEQ_LEN), bf16),
            pltpu.VMEM((width, SEQ_LEN), bf16),
            pltpu.VMEM((8, SEQ_LEN), f32),
            pltpu.VMEM((8, SEQ_LEN), f32),
            pltpu.SemaphoreType.DMA((3,)),
            pltpu.SemaphoreType.DMA((count,)),
            pltpu.SemaphoreType.DMA((len(carried),)),
        ],
        compiler_params=pltpu.CompilerParams(vmem_limit_bytes=ATTENTION_MIB * MIB),
        name="attention",
    )(in_hbm(tokens), in_hbm(qkv_weight), layer_biases, *[in_hbm(array) for array in carried])


def to_middle(block, tokens, context, out_weight, biases, gains):
    where = pl.ds(pl.multiple_of(block * SLICE, SLICE), SLICE)

    def rows(array):
        return array[:, where, :].reshape(-1, array.shape[2])

    attended = dot(rows(context), out_weight[...]) + biases[2:3]
    return norm_rows(rows(tokens).astype(f32) + attended, gains[0:1], biases[3:4]).astype(bf16)


def to_sums(middle, up_weight, down_weight, ffn_bias, biases):
    hidden = gelu(dot(middle, up_weight[...]) + ffn_bias[...].reshape(1, -1)).astype(bf16)
    return middle.astype(f32) + dot(hidden, down_weight[...]) + biases[4:5]


def to_layer(sums, biases, gains):
    return norm_rows(sums, gains[1:2], biases[5:6]).astype(bf16)


def orthonormal_rows(factor):
    index = lax.broadcasted_iota(jnp.int32, factor.shape, 0)
    for row in range(factor.shape[0]):
        vector = factor[row : row + 1]
        vector = vector * lax.rsqrt(jnp.sum(vector * vector, -1, keepdims=True) + 1e-06)
        along = jnp.sum(factor * vector, -1, keepdims=True)
        factor = jnp.where(index > row, factor - along * vector, factor)
        factor = jnp.where(index == row, vector, factor)
    return factor


def split(values):
    first = values.astype(bf16).astype(f32)
    second = (values - first).astype(bf16).astype(f32)
    return first, second, values - first - second


def stacked(values):
    return jnp.concatenate(split(values), 0).astype(bf16)


def folded(values):
    rows = values.shape[0] // 3
    return values[:rows] + values[rows : 2 * rows] + values[2 * rows :]


class Exchange:
    def __init__(self, slots, send_sem, recv_sem, me, count, device_of):
        self.slots, self.send_sem, self.recv_sem = slots, send_sem, recv_sem
        self.me, self.count, self.device_of = me, count, device_of

    def copy(self, step, slot, device):
        return pltpu.make_async_remote_copy(
            src_ref=self.slots.at[slot],
            dst_ref=self.slots.at[slot],
            send_sem=self.send_sem.at[step],
            recv_sem=self.recv_sem.at[slot],
            device_id=self.device_of(device),
            device_id_type=pl.DeviceIdType.MESH,
        )

    def greet(self, barrier):
        for step in range(1, self.count):
            pl.semaphore_signal(
                barrier,
                inc=1,
                device_id=self.device_of(lax.rem(self.me + step, self.count)),
                device_id_type=pl.DeviceIdType.MESH,
            )

    def start(self, value):
        self.slots[self.me] = value
        for step in range(1, self.count):
            self.copy(step, self.me, lax.rem(self.me + step, self.count)).start()

    def total(self):
        for step in range(1, self.count):
            source = lax.rem(self.me + self.count - step, self.count)
            self.copy(step, source, source).wait_recv()
            self.copy(step, self.me, lax.rem(self.me + step, self.count)).wait_send()
        total = self.slots[0]
        for other in range(1, self.count):
            total = total + self.slots[other]
        return total


def head_gradients(labels, first_rows, pool_weight, class_weight_t, ramp_biases):
    classes, width = class_weight_t.shape
    class_low = jnp.concatenate(
        [class_weight_t[...], jnp.zeros((LANES - classes, width), f32)], 0
    ).astype(bf16)
    biases = jnp.concatenate([ramp_biases[...], jnp.zeros((LANES - classes,), f32)], 0)
    biases = biases.reshape(1, -1)
    pre = dot(first_rows, pool_weight[...].astype(bf16)) + biases[:, :width]
    pooled = jnp.tanh(pre)
    pooled_low = pooled.astype(bf16)
    logits = dot(pooled_low, class_low, NT) + biases[:, width:]
    lane = lax.broadcasted_iota(jnp.int32, logits.shape, 1)
    row = lax.broadcasted_iota(jnp.int32, logits.shape, 0)
    target = jnp.full(logits.shape, -1, jnp.int32)
    for index in range(first_rows.shape[0] // ROW_TILE):
        target = jnp.where(row == index * ROW_TILE, labels[index], target)
    logits = jnp.where(lane < classes, logits, -jnp.inf)
    powers = jnp.exp(logits - jnp.max(logits, -1, keepdims=True))
    softened = powers / jnp.sum(powers, -1, keepdims=True)
    grad_logits = softened - (lane == target).astype(f32)
    grad_logits = jnp.where(row % ROW_TILE == 0, grad_logits, 0.0).astype(bf16)
    grad_class = dot(grad_logits, pooled_low, TN)[:8]
    grad_pooled = dot(grad_logits, class_low)
    grad_pre = (grad_pooled * (1.0 - pooled * pooled)).astype(bf16)
    bias_sum = jnp.sum(grad_pre.astype(f32), 0, keepdims=True)
    logit_sum = jnp.sum(grad_logits.astype(f32), 0, keepdims=True)
    logit_sum = jnp.concatenate([logit_sum, jnp.zeros((1, width - LANES), f32)], 1)
    index = lax.broadcasted_iota(jnp.int32, grad_class.shape, 0)
    head = jnp.where(index == classes, bias_sum, grad_class)
    return grad_pre, jnp.where(index == classes + 1, logit_sum, head)


def ramp_kernel(
    n_wide,
    n_narrow,
    labels,
    tokens,
    context,
    out_weight,
    up_weight,
    down_weight,
    ffn_bias,
    layer_biases,
    norm_gains,
    pool_weight,
    class_weight_t,
    ramp_biases,
    start_t,
    error,
    layer_part,
    middle_even,
    sums_odd,
    basis_out,
    factor_out,
    head_out,
    rows_out,
    grads_out,
    middle_odd,
    sums_even,
    error_high,
    error_low,
    factor_error,
    narrow_one,
    wide_one,
    narrow_two,
    wide_two,
    send_sem,
    recv_sem,
):
    turn = pl.program_id(0)
    wide, narrow = lax.axis_index("wide"), lax.axis_index("narrow")
    count, _, width = tokens.shape
    rank = start_t.shape[0]
    middle = (middle_even, middle_odd)
    sums = (sums_even, sums_odd)

    def group(index, slots, by_narrow):
        semaphores = send_sem.at[index], recv_sem.at[index]
        if by_narrow:
            return Exchange(slots, *semaphores, narrow, n_narrow, lambda i: (wide, i))
        return Exchange(slots, *semaphores, wide, n_wide, lambda i: (i, narrow))

    sum_one_narrow = group(0, narrow_one, True)
    sum_one_wide = group(1, wide_one, False)
    sum_two_narrow = group(2, narrow_two, True)
    sum_two_wide = group(3, wide_two, False)
    barrier = pltpu.get_barrier_semaphore()

    def middle_of(block, odd):
        middle[odd][...] = to_middle(
            block, tokens, context, out_weight, layer_biases, norm_gains
        )

    def step(index, odd):
        middle_of(index + 1, 1 - odd)
        sums[odd][...] = to_sums(
            middle[odd][...], up_weight, down_weight, ffn_bias, layer_biases
        )
        rows = to_layer(sums[1 - odd][...], layer_biases, norm_gains)
        layer_part[jnp.maximum(index - 1, 0)] = rows.reshape(count, SLICE, width)

    @pl.when(turn == 0)
    def _():
        sum_one_narrow.greet(barrier)
        sum_one_wide.greet(barrier)
        high = error[...].astype(bf16)
        low = (error[...] - high.astype(f32)).astype(bf16)
        error_high[...] = high
        error_low[...] = low
        start = stacked(start_t[...])
        factor_error[...] = folded(dot(start, high, NT) + dot(start, low, NT))
        middle_of(0, 0)
        sums_odd[...] = jnp.zeros_like(sums_odd)

    step(2 * turn, 0)

    @pl.when(turn == 0)
    def _():
        first = [sums_even[pl.ds(index * SLICE, ROW_TILE)] for index in range(count)]
        first_rows = to_layer(jnp.concatenate(first, 0), layer_biases, norm_gains)
        grads, head = head_gradients(
            labels, first_rows, pool_weight, class_weight_t, ramp_biases
        )
        inner = folded(dot(stacked(start_t[...]), grads, NT))
        factor = factor_error[...] + folded(dot(stacked(inner), first_rows))
        rows_out[...] = first_rows
        grads_out[...] = grads
        pl.semaphore_wait(barrier, n_narrow + n_wide - 2)
        sum_one_narrow.start(jnp.concatenate([factor, head], 0))

    @pl.when(turn == 2)
    def _():
        sum_two_wide.start(sum_two_narrow.total())

    step(2 * turn + 1, 1)

    @pl.when(turn == 0)
    def _():
        sum_one_wide.start(sum_one_narrow.total())

    @pl.when(turn == 1)
    def _():
        total = sum_one_wide.total()
        head_out[...] = total[rank:]
        basis = orthonormal_rows(total[:rank])
        basis_out[...] = basis
        basis = stacked(basis)
        inner = folded(dot(basis, rows_out[...], NT))
        factor = folded(dot(basis, error_high[...]) + dot(basis, error_low[...]))
        sum_two_narrow.start(factor + folded(dot(stacked(inner), grads_out[...])))

    @pl.when(turn == pl.num_programs(0) - 1)
    def _():
        factor_out[...] = sum_two_wide.total()


def ramp(n_wide, n_narrow, labels, tokens, context, *operands):
    start_t = operands[9]
    rank, width = start_t.shape
    count, length, _ = tokens.shape
    most = max(n_wide, n_narrow)
    vmem = pl.BlockSpec(memory_space=pltpu.VMEM)
    steps = length // SLICE - LATE_STEPS
    first = ROW_TILE * count
    outs = [
        pltpu.VMEM((steps - 1, count, SLICE, width), bf16),
        pltpu.VMEM((count * SLICE, width), bf16),
        pltpu.VMEM((count * SLICE, width), f32),
        pltpu.VMEM((rank, width), f32),
        pltpu.VMEM((rank, width), f32),
        pltpu.VMEM((8, width), f32),
        pltpu.VMEM((first, width), bf16),
        pltpu.VMEM((first, width), bf16),
    ]
    return pl.pallas_call(
        functools.partial(ramp_kernel, n_wide, n_narrow),
        grid=(steps // 2,),
        in_specs=[pl.BlockSpec(memory_space=pltpu.SMEM)] + [vmem] * (2 + len(operands)),
        out_specs=[vmem] * len(outs),
        out_shape=outs,
        scratch_shapes=[
            pltpu.VMEM((count * SLICE, width), bf16),
            pltpu.VMEM((count * SLICE, width), f32),
            pltpu.VMEM((width, width), bf16),
            pltpu.VMEM((width, width), bf16),
            pltpu.VMEM((rank, width), f32),
            pltpu.VMEM((n_narrow, rank + 8, width), f32),
            pltpu.VMEM((n_wide, rank + 8, width), f32),
            pltpu.VMEM((n_narrow, rank, width), f32),
            pltpu.VMEM((n_wide, rank, width), f32),
            pltpu.SemaphoreType.DMA((4, most)),
            pltpu.SemaphoreType.DMA((4, most)),
        ],
        compiler_params=pltpu.CompilerParams(
            vmem_limit_bytes=RAMP_MIB * MIB, collective_id=0, has_side_effects=True
        ),
        name="ramp",
    )(labels, tokens, context, *operands)


def finish_kernel(
    devices,
    tokens,
    context,
    layer_part,
    middle,
    sums,
    out_weight,
    up_weight,
    down_weight,
    ffn_bias,
    layer_biases,
    norm_gains,
    basis,
    factor,
    rows,
    grads,
    head,
    error,
    pool_weight,
    pool_moment,
    class_weight_t,
    class_moment_t,
    ramp_biases,
    bias_moment,
    layer_out,
    error_new,
    pool_weight_new,
    pool_moment_new,
    factor_new,
    class_weight_new,
    class_moment_new,
    ramp_biases_new,
    bias_moment_new,
    done,
    held,
    part_sem,
    done_sem,
    store_sem,
):
    ready, count, _, width = layer_part.shape
    classes = class_weight_t.shape[0]

    def block_of(array, index):
        return array.at[:, pl.ds(index * SLICE, SLICE)]

    parts = [
        pltpu.make_async_copy(layer_part.at[index], block_of(layer_out, index), part_sem.at[index])
        for index in range(ready)
    ]
    stores = [
        pltpu.make_async_copy(held.at[index], into, store_sem.at[index])
        for index, into in enumerate([error_new, pool_weight_new, pool_moment_new])
    ]

    def done_copy(index):
        into = block_of(layer_out, ready + index)
        return pltpu.make_async_copy(done.at[index], into, done_sem.at[index])

    def finish_block(index, values):
        done[index] = to_layer(values, layer_biases, norm_gains).reshape(count, SLICE, width)
        done_copy(index).start()

    for copy in parts:
        copy.start()
    finish_block(0, sums[...])
    high, mid, low = split(basis[...])
    left = jnp.concatenate([high, high, mid, mid, high, low], 0).astype(bf16)
    high, mid, low = split(factor[...])
    right = jnp.concatenate([high, mid, high, mid, low, high], 0).astype(bf16)
    approx = dot(left, right, TN)
    combined = dot(rows[...], grads[...], TN) + error[...]
    held[0] = combined - approx * (1.0 / devices)
    moment = MOMENTUM * pool_moment[...] + approx
    held[2] = moment
    held[1] = pool_weight[...] - RATE_POOL * moment
    for copy in stores:
        copy.start()
    factor_new[...] = factor[...]

    first_block = ready + 1
    middle = {first_block: middle[...]}
    for block in range(first_block, first_block + LATE_STEPS):
        if block + 1 < first_block + LATE_STEPS:
            middle[block + 1] = to_middle(
                block + 1, tokens, context, out_weight, layer_biases, norm_gains
            )
        next_sums = to_sums(middle[block], up_weight, down_weight, ffn_bias, layer_biases)
        finish_block(block - ready, next_sums)

    moment = MOMENTUM * class_moment_t[...] + head[:classes]
    class_moment_new[...] = moment
    class_weight_new[...] = class_weight_t[...] - RATE_HEAD * moment
    total = jnp.concatenate(
        [head[classes : classes + 1], head[classes + 1 : classes + 2, :classes]], 1
    )
    moment = MOMENTUM * bias_moment[...] + total.reshape(-1)
    bias_moment_new[...] = moment
    ramp_biases_new[...] = ramp_biases[...] - RATE_BIAS * moment

    for copy in parts + stores:
        copy.wait()
    for index in range(1 + LATE_STEPS):
        done_copy(index).wait()


def finish(devices, *operands):
    vmem = pl.BlockSpec(memory_space=pltpu.VMEM)
    hbm = pl.BlockSpec(memory_space=pltpu.HBM)
    tokens, layer_part, factor = operands[0], operands[2], operands[12]
    ready, *shape = layer_part.shape
    width = shape[-1]
    large = (tokens, *operands[16:19])
    small = (factor, *operands[19:])
    return pl.pallas_call(
        functools.partial(finish_kernel, devices),
        in_specs=[vmem] * len(operands),
        out_specs=[hbm] * len(large) + [vmem] * len(small),
        out_shape=[pltpu.HBM(array.shape, array.dtype) for array in large]
        + [jax.ShapeDtypeStruct(array.shape, array.dtype) for array in small],
        scratch_shapes=[
            pltpu.VMEM((1 + LATE_STEPS, *shape), bf16),
            pltpu.VMEM((3, width, width), f32),
            pltpu.SemaphoreType.DMA((ready,)),
            pltpu.SemaphoreType.DMA((1 + LATE_STEPS,)),
            pltpu.SemaphoreType.DMA((3,)),
        ],
        compiler_params=pltpu.CompilerParams(vmem_limit_bytes=FINISH_MIB * MIB),
        name="finish",
    )(*operands)


def body(
    n_wide,
    n_narrow,
    tokens,
    labels,
    qkv_weight,
    out_weight,
    up_weight,
    down_weight,
    ffn_bias,
    layer_biases,
    norm_gains,
    pool_weight,
    pool_moment,
    class_weight,
    class_moment,
    ramp_biases,
    bias_moment,
    start_factor,
    error_buffer,
):
    width = tokens.shape[1]
    carried = (
        out_weight,
        up_weight,
        down_weight,
        ffn_bias,
        layer_biases,
        norm_gains,
        error_buffer,
        pool_weight,
        pool_moment,
        class_weight.T,
        class_moment.T,
        ramp_biases,
        bias_moment,
        start_factor.T,
    )
    sequences, context, *carried = attention(tokens, qkv_weight, layer_biases, carried)
    layer = carried[:6]
    error, pool_weight, pool_moment, class_weight, class_moment = carried[6:11]
    ramp_biases, bias_moment, start = carried[11:]
    context = context.reshape(-1, SEQ_LEN, width)
    sequences = sequences.reshape(-1, SEQ_LEN, width)
    layer_part, middle, sums, basis, factor, head, first_rows, grads = ramp(
        n_wide,
        n_narrow,
        labels,
        sequences,
        context,
        *layer,
        pool_weight,
        class_weight,
        ramp_biases,
        start,
        error,
    )
    (
        layer_out,
        error_new,
        pool_weight_new,
        pool_moment_new,
        factor_new,
        class_weight_new,
        class_moment_new,
        ramp_biases_new,
        bias_moment_new,
    ) = finish(
        n_wide * n_narrow,
        sequences,
        context,
        layer_part,
        middle,
        sums,
        *layer,
        basis,
        factor,
        first_rows,
        grads,
        head,
        error,
        pool_weight,
        pool_moment,
        class_weight,
        class_moment,
        ramp_biases,
        bias_moment,
    )
    return (
        layer_out.reshape(tokens.shape),
        pool_moment_new,
        pool_weight_new,
        class_moment_new.T,
        class_weight_new.T,
        bias_moment_new,
        ramp_biases_new,
        error_new,
        factor_new.T,
    )


def solution(mesh):
    rows = P(("wide", "narrow"), None)
    in_specs = (rows, P(("wide", "narrow"))) + (P(),) * 14 + (rows,)
    out_specs = (rows,) + (P(),) * 6 + (rows, P())
    return jax.shard_map(
        functools.partial(body, mesh.shape["wide"], mesh.shape["narrow"]),
        mesh=mesh,
        in_specs=in_specs,
        out_specs=out_specs,
        check_vma=False,
    )
```

profile of v0, /device:TPU:0, one launch (start us, length us, event | category | flops | bytes accessed | tf_op | source)
XLA Modules:
  0.0 106.0 jit_solution(1293756962554545496)
XLA Ops:
  0.6 0.0 copy-start
  0.7 50.4 %attention.1 = (bf16[3072,768]{1,0:T(8,128)(2,1)S(1)}, bf16[3072,768]{1,0:T(8,128)(2,1)S(1)}, bf16[768,768]{1,0:T(8,128)(2,1)S(1)}, bf16[768,3072]{1,0:T(8,128)(...) custom-call(bf16[3072,768]{1,0:T(8,128)(2,1)} %tokens.1, ...), custom_call_target="tpu_custom_call" | custom-call | tf_op jit(solution)/shard_map/attention/pallas_call | solution.py:196
  51.1 0.0 copy-done
  51.1 41.0 %ramp.1 = (bf16[5,3,128,768]{3,2,1,0:T(8,128)(2,1)S(1)}, bf16[384,768]{1,0:T(8,128)(2,1)S(1)}, f32[384,768]{1,0:T(8,128)S(1)}, f32[8,768]{1,0:T(8,128)S(1)}, f32...) custom-call(s32[3]{0:T(128)S(1)} %copy-done, ...), custom_call_target="tpu_custom_call" | custom-call | tf_op jit(solution)/shard_map/ramp/pallas_call | solution.py:480
  92.0 13.8 %finish.1 = (bf16[3,1024,768]{2,1,0:T(8,128)(2,1)}, f32[768,768]{1,0:T(8,128)}, f32[768,768]{1,0:T(8,128)}, f32[768,768]{1,0:T(8,128)}, f32[8,768]{1,0:T(8,128)}...) custom-call(bf16[3,1024,768]{2,1,0:T(8,128)(2,1)S(1)} %bitcast.10, ...), custom_call_target="tpu_custom_call" | custom-call | tf_op jit(solution)/shard_map/finish/pallas_call | solution.py:620
Async XLA Ops:
  0.6 50.4 %copy-start = (s32[3]{0:T(128)S(1)}, s32[3]{0:T(128)}, u32[]{:S(2)}) copy-start(s32[3]{0:T(128)} %labels.1) | copy-start | bytes 40
where the time goes:
time: 106 us
  Pallas kernels  105 us (99%)
    pallas_call x1, Pallas kernels, attention(): pl.pallas_call(functools.partial(attention_kernel, len(carried)), grid=(c...  50.4 us
    pallas_call x1, Pallas kernels, ramp(): pl.pallas_call(functools.partial(ramp_kernel, n_wide, n_narrow), grid=(st...  41 us
    pallas_call x1, Pallas kernels, finish(): pl.pallas_call(functools.partial(finish_kernel, devices), in_specs=[vmem]...  13.8 us

commit v1 on v0

--- a/solution.py
+++ b/solution.py
@@ -15,7 +15,7 @@
 LANES = 128
 SLICE = 128
 LATE_STEPS = 2
-HEAD_GROUP = 4
+HEAD_GROUP = 6
 LOG2E = 1.4426950408889634
 SAFE = 2.0**100
 MOMENTUM = 0.9
@@ -396,13 +396,14 @@
             block, tokens, context, out_weight, layer_biases, norm_gains
         )
 
-    def step(index, odd):
-        middle_of(index + 1, 1 - odd)
+    def sums_of(odd):
         sums[odd][...] = to_sums(
             middle[odd][...], up_weight, down_weight, ffn_bias, layer_biases
         )
-        rows = to_layer(sums[1 - odd][...], layer_biases, norm_gains)
-        layer_part[jnp.maximum(index - 1, 0)] = rows.reshape(count, SLICE, width)
+
+    def layer_of(block, odd):
+        rows = to_layer(sums[odd][...], layer_biases, norm_gains)
+        layer_part[block] = rows.reshape(count, SLICE, width)
 
     @pl.when(turn == 0)
     def _():
@@ -417,7 +418,8 @@
         middle_of(0, 0)
         sums_odd[...] = jnp.zeros_like(sums_odd)
 
-    step(2 * turn, 0)
+    middle_of(2 * turn + 1, 1)
+    sums_of(0)
 
     @pl.when(turn == 0)
     def _():
@@ -437,7 +439,10 @@
     def _():
         sum_two_wide.start(sum_two_narrow.total())
 
-    step(2 * turn + 1, 1)
+    layer_of(jnp.maximum(2 * turn - 1, 0), 1)
+    middle_of(2 * turn + 2, 0)
+    sums_of(1)
+    layer_of(2 * turn, 0)
 
     @pl.when(turn == 0)
     def _():
@@ -558,13 +563,17 @@
         for index, into in enumerate([error_new, pool_weight_new, pool_moment_new])
     ]
 
-    def done_copy(index):
-        into = block_of(layer_out, ready + index)
-        return pltpu.make_async_copy(done.at[index], into, done_sem.at[index])
+    def done_copy(index, sequence):
+        into = layer_out.at[sequence, pl.ds((ready + index) * SLICE, SLICE)]
+        return pltpu.make_async_copy(
+            done.at[index, sequence], into, done_sem.at[index, sequence]
+        )
 
     def finish_block(index, values):
-        done[index] = to_layer(values, layer_biases, norm_gains).reshape(count, SLICE, width)
-        done_copy(index).start()
+        for sequence in range(count):
+            rows = values[sequence * SLICE : (sequence + 1) * SLICE]
+            done[index, sequence] = to_layer(rows, layer_biases, norm_gains)
+            done_copy(index, sequence).start()
 
     for copy in parts:
         copy.start()
@@ -606,7 +615,8 @@
     for copy in parts + stores:
         copy.wait()
     for index in range(1 + LATE_STEPS):
-        done_copy(index).wait()
+        for sequence in range(count):
+            done_copy(index, sequence).wait()
 
 
 def finish(devices, *operands):
@@ -627,7 +637,7 @@
             pltpu.VMEM((1 + LATE_STEPS, *shape), bf16),
             pltpu.VMEM((3, width, width), f32),
             pltpu.SemaphoreType.DMA((ready,)),
-            pltpu.SemaphoreType.DMA((1 + LATE_STEPS,)),
+            pltpu.SemaphoreType.DMA((1 + LATE_STEPS, shape[0])),
             pltpu.SemaphoreType.DMA((3,)),
         ],
         compiler_params=pltpu.CompilerParams(vmem_limit_bytes=FINISH_MIB * MIB),

time: 106 us -> 103 us (0.972)
  Pallas kernels: 105 us -> 102 us
    pallas_call x1, Pallas kernels: 13.8 us -> 11.6 us  [finish(): pl.pallas_call(functools.partial(finish_kernel, devices), in_specs=[vmem]...]
where the time goes in v1:
time: 103 us
  Pallas kernels  102 us (99%)
    pallas_call x1, Pallas kernels, attention(): pl.pallas_call(functools.partial(attention_kernel, len(carried)), grid=(c...  49.6 us
    pallas_call x1, Pallas kernels, ramp(): pl.pallas_call(functools.partial(ramp_kernel, n_wide, n_narrow), grid=(st...  40.7 us
    pallas_call x1, Pallas kernels, finish(): pl.pallas_call(functools.partial(finish_kernel, devices), in_specs=[vmem]...  11.6 us

profile of v1, /device:TPU:0, one launch (start us, length us, event | category | flops | bytes accessed | tf_op | source)
XLA Modules:
  0.0 102.7 jit_solution(3346078170491117997)
XLA Ops:
  0.6 0.0 copy-start
  0.7 49.6 %attention.1 = (bf16[3072,768]{1,0:T(8,128)(2,1)S(1)}, bf16[3072,768]{1,0:T(8,128)(2,1)S(1)}, bf16[768,768]{1,0:T(8,128)(2,1)S(1)}, bf16[768,3072]{1,0:T(8,128)(...) custom-call(bf16[3072,768]{1,0:T(8,128)(2,1)} %tokens.1, ...), custom_call_target="tpu_custom_call" | custom-call | tf_op jit(solution)/shard_map/attention/pallas_call | solution.py:196
  50.3 0.0 copy-done
  50.3 40.7 %ramp.1 = (bf16[5,3,128,768]{3,2,1,0:T(8,128)(2,1)S(1)}, bf16[384,768]{1,0:T(8,128)(2,1)S(1)}, f32[384,768]{1,0:T(8,128)S(1)}, f32[8,768]{1,0:T(8,128)S(1)}, f32...) custom-call(s32[3]{0:T(128)S(1)} %copy-done, ...), custom_call_target="tpu_custom_call" | custom-call | tf_op jit(solution)/shard_map/ramp/pallas_call | solution.py:485
  91.0 11.6 %finish.1 = (bf16[3,1024,768]{2,1,0:T(8,128)(2,1)}, f32[768,768]{1,0:T(8,128)}, f32[768,768]{1,0:T(8,128)}, f32[768,768]{1,0:T(8,128)}, f32[8,768]{1,0:T(8,128)}...) custom-call(bf16[3,1024,768]{2,1,0:T(8,128)(2,1)S(1)} %bitcast.10, ...), custom_call_target="tpu_custom_call" | custom-call | tf_op jit(solution)/shard_map/finish/pallas_call | solution.py:630
Async XLA Ops:
  0.6 49.6 %copy-start = (s32[3]{0:T(128)S(1)}, s32[3]{0:T(128)}, u32[]{:S(2)}) copy-start(s32[3]{0:T(128)} %labels.1) | copy-start | bytes 40

commit v2 on v1

--- a/solution.py
+++ b/solution.py
@@ -24,7 +24,7 @@
 RATE_BIAS = 0.03
 MIB = 1024 * 1024
 ATTENTION_MIB = 23
-RAMP_MIB = 12
+RAMP_MIB = 11.25
 FINISH_MIB = 14
 
 f32 = jnp.float32
@@ -82,7 +82,6 @@
         values_t,
         context_t,
         low,
-        high,
         weight_sem,
         token_sem,
         carry_sem,
@@ -115,9 +114,9 @@
 
     @pl.when(step == 0)
     def _():
+        token_copy(0).start()
         query_copy.start()
         value_copy.start()
-        token_copy(0).start()
         key_copy.start()
         columns = jnp.concatenate([layer_biases[...], jnp.zeros((2, width), f32)], 0).T
         query_bias[...] = jnp.broadcast_to(columns[:, 0:1], (width, LANES))
@@ -155,7 +154,6 @@
         values_t[head, :HEAD_DIM, :] = value_cols[own]
 
     low[...] = jnp.ones_like(low)
-    high[...] = jnp.ones_like(high)
 
     @pl.loop(0, heads // HEAD_GROUP)
     def _(group):
@@ -163,14 +161,13 @@
             head = group * HEAD_GROUP + offset
             sums = head_sums(dot(keys[head // 2], queries_t[head]), values_t[head], False)
             denominators = sums[HEAD_DIM : HEAD_DIM + 8]
-            low[...] = jnp.minimum(low[...], denominators)
-            high[...] = jnp.maximum(high[...], denominators)
+            low[...] = jnp.minimum(low[...], jnp.minimum(denominators, 1.0 / denominators))
             put_context(context_t, head, sums)
             if offset % 2:
                 lanes = pl.ds(pl.multiple_of((head // 2) * PAIR, PAIR), PAIR)
                 context[rows_of(step), lanes] = context_t[lanes, :].T
 
-    in_range = (jnp.min(low[...]) > 1.0 / SAFE) & (jnp.max(high[...]) < SAFE)
+    in_range = jnp.min(low[...]) > 1.0 / SAFE
 
     @pl.when(jnp.logical_not(in_range))
     def _():
@@ -208,7 +205,6 @@
             pltpu.VMEM((heads, V_ROWS, SEQ_LEN), bf16),
             pltpu.VMEM((width, SEQ_LEN), bf16),
             pltpu.VMEM((8, SEQ_LEN), f32),
-            pltpu.VMEM((8, SEQ_LEN), f32),
             pltpu.SemaphoreType.DMA((3,)),
             pltpu.SemaphoreType.DMA((count,)),
             pltpu.SemaphoreType.DMA((len(carried),)),
@@ -241,9 +237,10 @@
     index = lax.broadcasted_iota(jnp.int32, factor.shape, 0)
     for row in range(factor.shape[0]):
         vector = factor[row : row + 1]
-        vector = vector * lax.rsqrt(jnp.sum(vector * vector, -1, keepdims=True) + 1e-06)
         along = jnp.sum(factor * vector, -1, keepdims=True)
-        factor = jnp.where(index > row, factor - along * vector, factor)
+        scale = lax.rsqrt(along[row : row + 1] + 1e-06)
+        vector = vector * scale
+        factor = jnp.where(index > row, factor - along * scale * vector, factor)
         factor = jnp.where(index == row, vector, factor)
     return factor
 
@@ -354,7 +351,7 @@
     error,
     layer_part,
     middle_even,
-    sums_odd,
+    middle_last,
     basis_out,
     factor_out,
     head_out,
@@ -362,6 +359,7 @@
     grads_out,
     middle_odd,
     sums_even,
+    sums_odd,
     error_high,
     error_low,
     factor_error,
@@ -461,6 +459,11 @@
 
     @pl.when(turn == pl.num_programs(0) - 1)
     def _():
+        last = layer_part.shape[0] - 1
+        layer_of(last, 1)
+        middle_last[...] = to_middle(
+            last + 2, tokens, context, out_weight, layer_biases, norm_gains
+        )
         factor_out[...] = sum_two_wide.total()
 
 
@@ -473,15 +476,16 @@
     steps = length // SLICE - LATE_STEPS
     first = ROW_TILE * count
     outs = [
-        pltpu.VMEM((steps - 1, count, SLICE, width), bf16),
+        pltpu.VMEM((steps, count, SLICE, width), bf16),
         pltpu.VMEM((count * SLICE, width), bf16),
-        pltpu.VMEM((count * SLICE, width), f32),
+        pltpu.VMEM((count * SLICE, width), bf16),
         pltpu.VMEM((rank, width), f32),
         pltpu.VMEM((rank, width), f32),
         pltpu.VMEM((8, width), f32),
         pltpu.VMEM((first, width), bf16),
         pltpu.VMEM((first, width), bf16),
     ]
+    slots = (n_wide + n_narrow) * (2 * rank + 8) * width * 4
     return pl.pallas_call(
         functools.partial(ramp_kernel, n_wide, n_narrow),
         grid=(steps // 2,),
@@ -490,6 +494,7 @@
         out_shape=outs,
         scratch_shapes=[
             pltpu.VMEM((count * SLICE, width), bf16),
+            pltpu.VMEM((count * SLICE, width), f32),
             pltpu.VMEM((count * SLICE, width), f32),
             pltpu.VMEM((width, width), bf16),
             pltpu.VMEM((width, width), bf16),
@@ -502,7 +507,7 @@
             pltpu.SemaphoreType.DMA((4, most)),
         ],
         compiler_params=pltpu.CompilerParams(
-            vmem_limit_bytes=RAMP_MIB * MIB, collective_id=0, has_side_effects=True
+            vmem_limit_bytes=int(RAMP_MIB * MIB) + slots, collective_id=0, has_side_effects=True
         ),
         name="ramp",
     )(labels, tokens, context, *operands)
@@ -510,12 +515,9 @@
 
 def finish_kernel(
     devices,
-    tokens,
-    context,
     layer_part,
-    middle,
-    sums,
-    out_weight,
+    first_middle,
+    last_middle,
     up_weight,
     down_weight,
     ffn_bias,
@@ -577,7 +579,8 @@
 
     for copy in parts:
         copy.start()
-    finish_block(0, sums[...])
+    sums = to_sums(first_middle[...], up_weight, down_weight, ffn_bias, layer_biases)
+    finish_block(0, sums)
     high, mid, low = split(basis[...])
     left = jnp.concatenate([high, high, mid, mid, high, low], 0).astype(bf16)
     high, mid, low = split(factor[...])
@@ -592,15 +595,8 @@
         copy.start()
     factor_new[...] = factor[...]
 
-    first_block = ready + 1
-    middle = {first_block: middle[...]}
-    for block in range(first_block, first_block + LATE_STEPS):
-        if block + 1 < first_block + LATE_STEPS:
-            middle[block + 1] = to_middle(
-                block + 1, tokens, context, out_weight, layer_biases, norm_gains
-            )
-        next_sums = to_sums(middle[block], up_weight, down_weight, ffn_bias, layer_biases)
-        finish_block(block - ready, next_sums)
+    sums = to_sums(last_middle[...], up_weight, down_weight, ffn_bias, layer_biases)
+    finish_block(1, sums)
 
     moment = MOMENTUM * class_moment_t[...] + head[:classes]
     class_moment_new[...] = moment
@@ -614,19 +610,19 @@
 
     for copy in parts + stores:
         copy.wait()
-    for index in range(1 + LATE_STEPS):
+    for index in range(LATE_STEPS):
         for sequence in range(count):
             done_copy(index, sequence).wait()
 
 
-def finish(devices, *operands):
+def finish(devices, tokens, *operands):
     vmem = pl.BlockSpec(memory_space=pltpu.VMEM)
     hbm = pl.BlockSpec(memory_space=pltpu.HBM)
-    tokens, layer_part, factor = operands[0], operands[2], operands[12]
+    layer_part, factor = operands[0], operands[9]
     ready, *shape = layer_part.shape
     width = shape[-1]
-    large = (tokens, *operands[16:19])
-    small = (factor, *operands[19:])
+    large = (tokens, *operands[13:16])
+    small = (factor, *operands[16:])
     return pl.pallas_call(
         functools.partial(finish_kernel, devices),
         in_specs=[vmem] * len(operands),
@@ -634,10 +630,10 @@
         out_shape=[pltpu.HBM(array.shape, array.dtype) for array in large]
         + [jax.ShapeDtypeStruct(array.shape, array.dtype) for array in small],
         scratch_shapes=[
-            pltpu.VMEM((1 + LATE_STEPS, *shape), bf16),
+            pltpu.VMEM((LATE_STEPS, *shape), bf16),
             pltpu.VMEM((3, width, width), f32),
             pltpu.SemaphoreType.DMA((ready,)),
-            pltpu.SemaphoreType.DMA((1 + LATE_STEPS, shape[0])),
+            pltpu.SemaphoreType.DMA((LATE_STEPS, shape[0])),
             pltpu.SemaphoreType.DMA((3,)),
         ],
         compiler_params=pltpu.CompilerParams(vmem_limit_bytes=FINISH_MIB * MIB),
@@ -689,7 +685,7 @@
     ramp_biases, bias_moment, start = carried[11:]
     context = context.reshape(-1, SEQ_LEN, width)
     sequences = sequences.reshape(-1, SEQ_LEN, width)
-    layer_part, middle, sums, basis, factor, head, first_rows, grads = ramp(
+    layer_part, middle, last_middle, basis, factor, head, first_rows, grads = ramp(
         n_wide,
         n_narrow,
         labels,
@@ -715,11 +711,10 @@
     ) = finish(
         n_wide * n_narrow,
         sequences,
-        context,
         layer_part,
         middle,
-        sums,
-        *layer,
+        last_middle,
+        *layer[1:],
         basis,
         factor,
         first_rows,

time: 103 us -> 102 us (level)
  no operation moved by 1% of the time
where the time goes in v2:
time: 102 us; the launch traced here: 101 us
  Pallas kernels  101 us (99%)
    pallas_call x1, Pallas kernels, attention(): pl.pallas_call(functools.partial(attention_kernel, len(carried)), grid=(c...  49.4 us
    pallas_call x1, Pallas kernels, ramp(): pl.pallas_call(functools.partial(ramp_kernel, n_wide, n_narrow), grid=(st...  40.2 us
    pallas_call x1, Pallas kernels, finish(): pl.pallas_call(functools.partial(finish_kernel, devices), in_specs=[vmem]...  11 us

profile of v2, /device:TPU:0, one launch (start us, length us, event | category | flops | bytes accessed | tf_op | source)
XLA Modules:
  0.0 101.4 jit_solution(127691520529979683)
XLA Ops:
  0.7 0.0 copy-start
  0.7 49.4 %attention.1 = (bf16[3072,768]{1,0:T(8,128)(2,1)S(1)}, bf16[3072,768]{1,0:T(8,128)(2,1)S(1)}, bf16[768,768]{1,0:T(8,128)(2,1)S(1)}, bf16[768,3072]{1,0:T(8,128)(...) custom-call(bf16[3072,768]{1,0:T(8,128)(2,1)} %tokens.1, ...), custom_call_target="tpu_custom_call" | custom-call | tf_op jit(solution)/shard_map/attention/pallas_call | solution.py:193
  50.1 0.0 copy-done
  50.1 40.2 %ramp.1 = (bf16[6,3,128,768]{3,2,1,0:T(8,128)(2,1)S(1)}, bf16[384,768]{1,0:T(8,128)(2,1)S(1)}, bf16[384,768]{1,0:T(8,128)(2,1)S(1)}, f32[8,768]{1,0:T(8,128)S(1)...) custom-call(s32[3]{0:T(128)S(1)} %copy-done, ...), custom_call_target="tpu_custom_call" | custom-call | tf_op jit(solution)/shard_map/ramp/pallas_call | solution.py:489
  90.3 11.0 %finish.1 = (bf16[3,1024,768]{2,1,0:T(8,128)(2,1)}, f32[768,768]{1,0:T(8,128)}, f32[768,768]{1,0:T(8,128)}, f32[768,768]{1,0:T(8,128)}, f32[8,768]{1,0:T(8,128)}...) custom-call(bf16[6,3,128,768]{3,2,1,0:T(8,128)(2,1)S(1)} %get-tuple-element.55.layer_part, ...), custom_call_target="tpu_custom_call" | custom-call | tf_op jit(solution)/shard_map/finish/pallas_call | solution.py:626
Async XLA Ops:
  0.7 49.5 %copy-start = (s32[3]{0:T(128)S(1)}, s32[3]{0:T(128)}, u32[]{:S(2)}) copy-start(s32[3]{0:T(128)} %labels.1) | copy-start | bytes 40

commit v3 on v2

--- a/solution.py
+++ b/solution.py
@@ -437,8 +437,8 @@
     def _():
         sum_two_wide.start(sum_two_narrow.total())
 
+    middle_of(2 * turn + 2, 0)
     layer_of(jnp.maximum(2 * turn - 1, 0), 1)
-    middle_of(2 * turn + 2, 0)
     sums_of(1)
     layer_of(2 * turn, 0)
 

time: 102 us -> 102 us (level)
  no operation moved by 1% of the time
where the time goes in v3:
time: 102 us; the launch traced here: 101 us
  Pallas kernels  101 us (99%)
    pallas_call x1, Pallas kernels, attention(): pl.pallas_call(functools.partial(attention_kernel, len(carried)), grid=(c...  49.4 us
    pallas_call x1, Pallas kernels, ramp(): pl.pallas_call(functools.partial(ramp_kernel, n_wide, n_narrow), grid=(st...  40.1 us
    pallas_call x1, Pallas kernels, finish(): pl.pallas_call(functools.partial(finish_kernel, devices), in_specs=[vmem]...  11 us

profile of v3, /device:TPU:0, one launch (start us, length us, event | category | flops | bytes accessed | tf_op | source)
XLA Modules:
  0.0 101.4 jit_solution(10895418412201413527)
XLA Ops:
  0.7 0.0 copy-start
  0.7 49.4 %attention.1 = (bf16[3072,768]{1,0:T(8,128)(2,1)S(1)}, bf16[3072,768]{1,0:T(8,128)(2,1)S(1)}, bf16[768,768]{1,0:T(8,128)(2,1)S(1)}, bf16[768,3072]{1,0:T(8,128)(...) custom-call(bf16[3072,768]{1,0:T(8,128)(2,1)} %tokens.1, ...), custom_call_target="tpu_custom_call" | custom-call | tf_op jit(solution)/shard_map/attention/pallas_call | solution.py:193
  50.1 0.0 copy-done
  50.1 40.1 %ramp.1 = (bf16[6,3,128,768]{3,2,1,0:T(8,128)(2,1)S(1)}, bf16[384,768]{1,0:T(8,128)(2,1)S(1)}, bf16[384,768]{1,0:T(8,128)(2,1)S(1)}, f32[8,768]{1,0:T(8,128)S(1)...) custom-call(s32[3]{0:T(128)S(1)} %copy-done, ...), custom_call_target="tpu_custom_call" | custom-call | tf_op jit(solution)/shard_map/ramp/pallas_call | solution.py:489
  90.2 11.0 %finish.1 = (bf16[3,1024,768]{2,1,0:T(8,128)(2,1)}, f32[768,768]{1,0:T(8,128)}, f32[768,768]{1,0:T(8,128)}, f32[768,768]{1,0:T(8,128)}, f32[8,768]{1,0:T(8,128)}...) custom-call(bf16[6,3,128,768]{3,2,1,0:T(8,128)(2,1)S(1)} %get-tuple-element.55.layer_part, ...), custom_call_target="tpu_custom_call" | custom-call | tf_op jit(solution)/shard_map/finish/pallas_call | solution.py:626
Async XLA Ops:
  0.7 49.5 %copy-start = (s32[3]{0:T(128)S(1)}, s32[3]{0:T(128)}, u32[]{:S(2)}) copy-start(s32[3]{0:T(128)} %labels.1) | copy-start | bytes 40
